TPU v7x, 512 devices: a whole 4x4x16 slice. The times are simulated.
512 devices in a mesh: pts: 64 (over x, z_hi, y, core), freq: 8 (over z_lo).
Axes of the slice: x: 4, y: 4, z: 16 (z_hi: 2, z_lo: 8; z = z_hi * 8 + z_lo), core: 2. Of those that a mesh axis runs over, the one named last changes fastest.
Arguments:
- green_src: bfloat16 [24, 2, 128, 16384], P('freq', None, None, 'pts'), may hold values from -1.5 to 1.5
- green_rcv: bfloat16 [24, 2, 128, 16384], P('freq', None, None, 'pts'), may hold values from -1.5 to 1.5
- pairing: int32 [2, 64], replicated, may hold values from 0 to 63, as said below
- freq_index: int32 [24], P('freq'), may hold values from 32 to 63
Outputs:
- hessian: float32 [16384, 2, 256], P(('pts', 'freq'))
Inputs may be any that keep to these rules, and one draw needn't show every extreme that they name: Each row pairs the point blocks two by two: pairing[r, pairing[r, b]] = b and pairing[r, b] != b.
All inputs are finite; a program needn't handle non-finite values.
Results may differ from a plain program's by a relative error of at most 0.0003.
Values may be sent and summed in bfloat16 or wider, within the bound.
A program may use at most 64 MiB of HBM per device.

v0:
```python
from functools import partial

import jax
import jax.numpy as jnp
from jax import lax
from jax.sharding import PartitionSpec as P

ROUNDS = 2
FBINS = 64


def right_side(block):
    first = jnp.concatenate([block[:, 0], block[:, 1]], axis=1)
    second = jnp.concatenate([block[:, 1], -block[:, 0]], axis=1)
    return jnp.concatenate([first, second], axis=2)


def partial_rows(start, count, sources, receivers, right_src, right_rcv, weights):
    cols = right_src.shape[2] // 2
    total = jnp.zeros((count, cols), jnp.float32)
    for freq_slot in range(sources.shape[0]):
        left_s = sources[freq_slot]
        left_s = left_s.reshape(2 * sources.shape[2], count)
        left_r = receivers[freq_slot]
        left_r = left_r.reshape(2 * receivers.shape[2], count)
        prod_s = lax.dot_general(
            left_s,
            right_src[freq_slot],
            (((0,), (0,)), ((), ())),
            preferred_element_type=jnp.float32,
        )
        prod_r = lax.dot_general(
            left_r,
            right_rcv[freq_slot],
            (((0,), (0,)), ((), ())),
            preferred_element_type=jnp.float32,
        )
        total = total + weights[freq_slot] * (
            prod_s[:, :cols] * prod_r[:, :cols] - prod_s[:, cols:] * prod_r[:, cols:]
        )
    return total


def on_device(green_src, green_rcv, pairing, freq_index):
    points = green_src.shape[3]
    weights = ((freq_index.astype(jnp.float32) + 1.0) / FBINS) ** 4
    owned = points // lax.axis_size("freq")
    mates = []
    for step in range(ROUNDS):
        spread_s, spread_r = (
            lax.all_to_all(green_src[None], "pts", split_axis=3, concat_axis=0, tiled=True),
            lax.all_to_all(green_rcv[None], "pts", split_axis=3, concat_axis=0, tiled=True),
        )
        picked_s = jnp.take(spread_s, pairing[step], axis=0)
        picked_r = jnp.take(spread_r, pairing[step], axis=0)
        back_s, back_r = (
            lax.all_to_all(picked_s, "pts", split_axis=0, concat_axis=3, tiled=True),
            lax.all_to_all(picked_r, "pts", split_axis=0, concat_axis=3, tiled=True),
        )
        mates.append((right_side(back_s[0]), right_side(back_r[0])))
    results = []
    for step in range(ROUNDS):
        term = partial(
            partial_rows,
            sources=green_src,
            receivers=green_rcv,
            right_src=mates[step][0],
            right_rcv=mates[step][1],
            weights=weights,
        )
        results.append(
            lax.psum_scatter(
                term(jnp.int32(0), owned * lax.axis_size("freq")),
                "freq",
                scatter_dimension=0,
                tiled=True,
            )
        )
    hessian = jnp.stack(results, axis=1)
    return hessian


def solution(mesh):
    in_specs = (P("freq", None, None, "pts"), P("freq", None, None, "pts"), P(), P("freq"))
    out_specs = P(("pts", "freq"), None, None)
    return jax.shard_map(
        on_device, mesh=mesh, in_specs=in_specs, out_specs=out_specs, check_vma=False
    )
```

profile of v0, /device:TPU:24, one launch (start us, length us, event | category | flops | bytes accessed | tf_op | source)
XLA Modules:
  0.0 324.4 jit_solution(4547223277341594325)
XLA Ops:
  6.5 2.2 copy.88
  8.7 21.0 %all-to-all-start = ((bf16[1,3,2,128,256]{4,2,1,0,3:T(2,128)(2,1)}), bf16[1,3,2,128,256]{4,2,1,0,3:T(2,128)(2,1)S(1)}, u32[]{:S(2)}, u32[]{:S(2)}) async-start(bf16[1,3,2,128,256]{4,2,1,0,3:T(2,128)(2,1)} %bitcast.144), calls=%async_computation | async-start | bytes 786432 | tf_op jit(solution)/shard_map/all_to_all | solution.py:51
  30.9 17.0 %all-to-all-done = bf16[1,3,2,128,256]{4,2,1,0,3:T(2,128)(2,1)S(1)} async-done(((bf16[1,3,2,128,256]{4,2,1,0,3:T(2,128)(2,1)}), bf16[1,3,2,128,256]{4,2,1,0,3:T(2,128)(2,1)S(1)}, u32[]{:S(2)}, u32[]{:S(2)}) %all-to-all-start) | async-done | bytes 393248 | tf_op jit(solution)/shard_map/all_to_all | solution.py:51
  47.8 6.8 %all-to-all-start.2 = ((bf16[1,3,2,128,256]{4,2,1,0,3:T(2,128)(2,1)}), bf16[1,3,2,128,256]{4,2,1,0,3:T(2,128)(2,1)S(1)}, u32[]{:S(2)}, u32[]{:S(2)}) async-start(bf16[1,3,2,128,256]{4,2,1,0,3:T(2,128)(2,1)} %bitcast.143), calls=%async_computation.2 | async-start | bytes 786432 | tf_op jit(solution)/shard_map/all_to_all | solution.py:52
  55.1 17.5 %all-to-all-done.2 = bf16[1,3,2,128,256]{4,2,1,0,3:T(2,128)(2,1)S(1)} async-done(((bf16[1,3,2,128,256]{4,2,1,0,3:T(2,128)(2,1)}), bf16[1,3,2,128,256]{4,2,1,0,3:T(2,128)(2,1)S(1)}, u32[]{:S(2)}, u32[]{:S(2)}) %all-to-all-start.2) | async-done | bytes 393248 | tf_op jit(solution)/shard_map/all_to_all | solution.py:52
  73.0 1.4 gather_fusion
  75.7 1.7 broadcast_select_fusion.3
  77.4 6.7 %all-to-all-start.3 = ((bf16[64,3,2,2,256]{4,3,2,1,0:T(2,128)(2,1)}), bf16[64,3,2,2,256]{4,3,2,1,0:T(2,128)(2,1)S(1)}, u32[]{:S(2)}, u32[]{:S(2)}) async-start(bf16[64,3,2,2,256]{4,3,2,1,0:T(2,128)(2,1)} %get-tuple-element.35), calls=%async_computation.3 | async-start | bytes 786432 | tf_op jit(solution)/shard_map/all_to_all | solution.py:58
  84.1 17.8 %all-to-all-done.3 = bf16[64,3,2,2,256]{4,3,2,1,0:T(2,128)(2,1)S(1)} async-done(((bf16[64,3,2,2,256]{4,3,2,1,0:T(2,128)(2,1)}), bf16[64,3,2,2,256]{4,3,2,1,0:T(2,128)(2,1)S(1)}, u32[]{:S(2)}, u32[]{:S(2)}) %all-to-all-start.3) | async-done | bytes 393248 | tf_op jit(solution)/shard_map/all_to_all | solution.py:58
  102.0 6.7 %all-to-all-start.1 = ((bf16[64,3,2,2,256]{4,3,2,1,0:T(2,128)(2,1)}), bf16[64,3,2,2,256]{4,3,2,1,0:T(2,128)(2,1)S(1)}, u32[]{:S(2)}, u32[]{:S(2)}) async-start(bf16[64,3,2,2,256]{4,3,2,1,0:T(2,128)(2,1)} %get-tuple-element.34), calls=%async_computation.1 | async-start | bytes 786432 | tf_op jit(solution)/shard_map/all_to_all | solution.py:57
  110.2 1.4 gather_fusion.2
  111.5 1.4 gather_fusion.3
  112.9 1.7 broadcast_select_fusion.1
  115.6 10.9 %all-to-all-done.1 = bf16[64,3,2,2,256]{4,3,2,1,0:T(2,128)(2,1)S(1)} async-done(((bf16[64,3,2,2,256]{4,3,2,1,0:T(2,128)(2,1)}), bf16[64,3,2,2,256]{4,3,2,1,0:T(2,128)(2,1)S(1)}, u32[]{:S(2)}, u32[]{:S(2)}) %all-to-all-start.1) | async-done | bytes 393248 | tf_op jit(solution)/shard_map/all_to_all | solution.py:57
  126.6 10.6 %all-to-all-start.4 = ((bf16[64,3,2,2,256]{4,3,2,1,0:T(2,128)(2,1)}), bf16[64,3,2,2,256]{4,3,2,1,0:T(2,128)(2,1)S(1)}, u32[]{:S(2)}, u32[]{:S(2)}) async-start(bf16[64,3,2,2,256]{4,3,2,1,0:T(2,128)(2,1)} %get-tuple-element.39), calls=%async_computation.4 | async-start | bytes 786432 | tf_op jit(solution)/shard_map/all_to_all | solution.py:57
  140.4 14.7 %all-to-all-done.4 = bf16[64,3,2,2,256]{4,3,2,1,0:T(2,128)(2,1)S(1)} async-done(((bf16[64,3,2,2,256]{4,3,2,1,0:T(2,128)(2,1)}), bf16[64,3,2,2,256]{4,3,2,1,0:T(2,128)(2,1)S(1)}, u32[]{:S(2)}, u32[]{:S(2)}) %all-to-all-start.4) | async-done | bytes 393248 | tf_op jit(solution)/shard_map/all_to_all | solution.py:57
  155.0 7.3 %all-to-all-start.5 = ((bf16[64,3,2,2,256]{4,3,2,1,0:T(2,128)(2,1)}), bf16[64,3,2,2,256]{4,3,2,1,0:T(2,128)(2,1)}, u32[]{:S(2)}, u32[]{:S(2)}) async-start(bf16[64,3,2,2,256]{4,3,2,1,0:T(2,128)(2,1)} %get-tuple-element.40), calls=%async_computation.5 | async-start | bytes 786432 | tf_op jit(solution)/shard_map/all_to_all | solution.py:58
  162.4 2.8 fusion.10
  165.2 1.8 copy.57
  170.4 9.8 %all-to-all-done.5 = bf16[64,3,2,2,256]{4,3,2,1,0:T(2,128)(2,1)} async-done(((bf16[64,3,2,2,256]{4,3,2,1,0:T(2,128)(2,1)}), bf16[64,3,2,2,256]{4,3,2,1,0:T(2,128)(2,1)}, u32[]{:S(2)}, u32[]{:S(2)}) %all-to-all-start.5) | async-done | bytes 393248 | tf_op jit(solution)/shard_map/all_to_all | solution.py:58
  180.2 1.4 copy.51
  184.6 2.1 fusion.2
  187.5 68.1 %reduce-scatter.7.cloned.1.call-done = f32[32,256]{1,0:T(8,128)} async-done(((f32[256,256]{1,0:T(8,128)}), f32[32,256]{1,0:T(8,128)}) %reduce-scatter.7.cloned.1.call-update) | async-done | bytes 32784
  256.4 59.6 %reduce-scatter.9.cloned.1.call-done = f32[32,256]{1,0:T(8,128)} async-done(((f32[256,256]{1,0:T(8,128)}), f32[32,256]{1,0:T(8,128)}) %reduce-scatter.9.cloned.1.call-update) | async-done | bytes 32784
  (83 shorter events, 18.5 us)
Async XLA Ops:
  6.5 23.2 %copy-start = (bf16[3,2,128,256]{3,2,1,0:T(8,128)(2,1)S(1)}, bf16[3,2,128,256]{3,2,1,0:T(8,128)(2,1)}, u32[]{:S(2)}) copy-start(bf16[3,2,128,256]{3,2,1,0:T(8,128)(2,1)} %param.7) | copy-start | bytes 1179652
  8.7 39.1 %all-to-all-start = ((bf16[1,3,2,128,256]{4,2,1,0,3:T(2,128)(2,1)}), bf16[1,3,2,128,256]{4,2,1,0,3:T(2,128)(2,1)S(1)}, u32[]{:S(2)}, u32[]{:S(2)}) async-start(bf16[1,3,2,128,256]{4,2,1,0,3:T(2,128)(2,1)} %bitcast.144), calls=%async_computation | async-start | bytes 786432 | tf_op jit(solution)/shard_map/all_to_all | solution.py:51
  29.7 24.9 %copy-start.14 = (s32[2,64]{1,0:T(2,128)S(1)}, s32[2,64]{1,0:T(2,128)}, u32[]{:S(2)}) copy-start(s32[2,64]{1,0:T(2,128)} %param.8) | copy-start | bytes 1540
  47.8 24.7 %all-to-all-start.2 = ((bf16[1,3,2,128,256]{4,2,1,0,3:T(2,128)(2,1)}), bf16[1,3,2,128,256]{4,2,1,0,3:T(2,128)(2,1)S(1)}, u32[]{:S(2)}, u32[]{:S(2)}) async-start(bf16[1,3,2,128,256]{4,2,1,0,3:T(2,128)(2,1)} %bitcast.143), calls=%async_computation.2 | async-start | bytes 786432 | tf_op jit(solution)/shard_map/all_to_all | solution.py:52
  77.4 31.3 %copy-start.15 = (s32[3]{0:T(128)S(1)}, s32[3]{0:T(128)}, u32[]{:S(2)}) copy-start(s32[3]{0:T(128)} %param.9) | copy-start | bytes 40
  77.4 24.6 %all-to-all-start.3 = ((bf16[64,3,2,2,256]{4,3,2,1,0:T(2,128)(2,1)}), bf16[64,3,2,2,256]{4,3,2,1,0:T(2,128)(2,1)S(1)}, u32[]{:S(2)}, u32[]{:S(2)}) async-start(bf16[64,3,2,2,256]{4,3,2,1,0:T(2,128)(2,1)} %get-tuple-element.35), calls=%async_computation.3 | async-start | bytes 786432 | tf_op jit(solution)/shard_map/all_to_all | solution.py:58
  102.0 7.4 %copy-start.1 = (bf16[3,2,128,256]{3,2,1,0:T(8,128)(2,1)S(1)}, bf16[3,2,128,256]{3,2,1,0:T(8,128)(2,1)}, u32[]{:S(2)}) copy-start(bf16[3,2,128,256]{3,2,1,0:T(8,128)(2,1)} %param.6) | copy-start | bytes 1179652
  102.0 24.6 %all-to-all-start.1 = ((bf16[64,3,2,2,256]{4,3,2,1,0:T(2,128)(2,1)}), bf16[64,3,2,2,256]{4,3,2,1,0:T(2,128)(2,1)S(1)}, u32[]{:S(2)}, u32[]{:S(2)}) async-start(bf16[64,3,2,2,256]{4,3,2,1,0:T(2,128)(2,1)} %get-tuple-element.34), calls=%async_computation.1 | async-start | bytes 786432 | tf_op jit(solution)/shard_map/all_to_all | solution.py:57
  109.4 29.0 %copy-start.4 = (bf16[1,2,128,256]{3,2,1,0:T(8,128)(2,1)}, bf16[1,2,128,256]{3,2,1,0:T(8,128)(2,1)S(1)}, u32[]{:S(2)}) copy-start(bf16[1,2,128,256]{3,2,1,0:T(8,128)(2,1)S(1)} %get-tuple-element.25) | copy-start | bytes 393220
  109.4 29.2 %copy-start.2 = (bf16[1,2,128,256]{3,2,1,0:T(8,128)(2,1)}, bf16[1,2,128,256]{3,2,1,0:T(8,128)(2,1)S(1)}, u32[]{:S(2)}) copy-start(bf16[1,2,128,256]{3,2,1,0:T(8,128)(2,1)S(1)} %get-tuple-element.26) | copy-start | bytes 393220
  109.4 30.1 %copy-start.6 = (bf16[1,2,128,256]{3,2,1,0:T(8,128)(2,1)}, bf16[1,2,128,256]{3,2,1,0:T(8,128)(2,1)S(1)}, u32[]{:S(2)}) copy-start(bf16[1,2,128,256]{3,2,1,0:T(8,128)(2,1)S(1)} %get-tuple-element.27) | copy-start | bytes 393220
  110.2 28.7 %copy-start.10 = (bf16[1,2,128,256]{3,2,1,0:T(8,128)(2,1)}, bf16[1,2,128,256]{3,2,1,0:T(8,128)(2,1)S(1)}, u32[]{:S(2)}) copy-start(bf16[1,2,128,256]{3,2,1,0:T(8,128)(2,1)S(1)} %get-tuple-element.22) | copy-start | bytes 393220
  110.2 29.0 %copy-start.8 = (bf16[1,2,128,256]{3,2,1,0:T(8,128)(2,1)}, bf16[1,2,128,256]{3,2,1,0:T(8,128)(2,1)S(1)}, u32[]{:S(2)}) copy-start(bf16[1,2,128,256]{3,2,1,0:T(8,128)(2,1)S(1)} %get-tuple-element.23) | copy-start | bytes 393220
  126.6 28.5 %all-to-all-start.4 = ((bf16[64,3,2,2,256]{4,3,2,1,0:T(2,128)(2,1)}), bf16[64,3,2,2,256]{4,3,2,1,0:T(2,128)(2,1)S(1)}, u32[]{:S(2)}, u32[]{:S(2)}) async-start(bf16[64,3,2,2,256]{4,3,2,1,0:T(2,128)(2,1)} %get-tuple-element.39), calls=%async_computation.4 | async-start | bytes 786432 | tf_op jit(solution)/shard_map/all_to_all | solution.py:57
  139.2 0.9 copy-start.12
  155.0 25.1 %all-to-all-start.5 = ((bf16[64,3,2,2,256]{4,3,2,1,0:T(2,128)(2,1)}), bf16[64,3,2,2,256]{4,3,2,1,0:T(2,128)(2,1)}, u32[]{:S(2)}, u32[]{:S(2)}) async-start(bf16[64,3,2,2,256]{4,3,2,1,0:T(2,128)(2,1)} %get-tuple-element.40), calls=%async_computation.5 | async-start | bytes 786432 | tf_op jit(solution)/shard_map/all_to_all | solution.py:58
  162.3 93.2 %reduce-scatter.7.cloned.1.call-start = ((), (), s32[]{:S(2)}) async-start(), calls=%async_computation.8 | async-start | bytes 294912
  167.0 149.0 %reduce-scatter.9.cloned.1.call-start = ((), (), s32[]{:S(2)}) async-start(), calls=%async_computation.9 | async-start | bytes 294912
  168.1 0.9 copy-start.13
  169.0 0.9 copy-start.11
  169.0 1.2 copy-start.9
  182.2 0.9 copy-start.7
  183.1 0.9 copy-start.5
  183.1 1.2 copy-start.3
Sparse Core Ops, SparseCore 0:
  167.1 88.4 reduce-scatter.6
  258.6 57.3 reduce-scatter.8
where the time goes:
time: 326 us; the launch traced here: 324 us
  waiting for transfers between devices  215 us (66%)
  starting transfers between devices  59.2 us (18%)
  local copies, waits for them, and re-layouts  24.3 us (7%)
  between operations  13.9 us (4%)
  other arithmetic  8.6 us (3%)
    unnamed x4, waiting for transfers between devices  128 us
    all_to_all x2, waiting for transfers between devices, on_device(): lax.all_to_all(picked_r, 'pts', split_axis=0, concat_axis=3, tiled=True)  27.6 us
    all_to_all x2, waiting for transfers between devices, on_device(): lax.all_to_all(picked_s, 'pts', split_axis=0, concat_axis=3, tiled=True)  25.6 us
    all_to_all x1, starting transfers between devices, on_device(): lax.all_to_all(green_src[None], 'pts', split_axis=3, concat_axis=0, tiled...  21 us
    all_to_all x1, waiting for transfers between devices, on_device(): lax.all_to_all(green_rcv[None], 'pts', split_axis=3, concat_axis=0, tiled...  17.5 us
    all_to_all x2, starting transfers between devices, on_device(): lax.all_to_all(picked_s, 'pts', split_axis=0, concat_axis=3, tiled=True)  17.3 us
    all_to_all x1, waiting for transfers between devices, on_device(): lax.all_to_all(green_src[None], 'pts', split_axis=3, concat_axis=0, tiled...  17 us
    all_to_all x2, starting transfers between devices, on_device(): lax.all_to_all(picked_r, 'pts', split_axis=0, concat_axis=3, tiled=True)  14 us
  transfers between devices with their start and end apart: 8, of which 8 were waited for; matrix products, arithmetic and copies ran while one was open for 7% of the time, Pallas kernels for 0%

commit v1 on v0

v1 whole, which is shorter than its diff:
```python
import functools

import jax
import jax.numpy as jnp
from jax import lax
from jax.experimental import pallas as pl
from jax.experimental.pallas import tpu as pltpu
from jax.sharding import PartitionSpec as P

ROUNDS = 2
FBINS = 64
PEERS = 32
SLICE = 16
MESH = pl.DeviceIdType.MESH
CHUNKS = ((1, 0, 256), (0, 0, 128), (0, 128, 128))


def device(x, y_core, z):
    return (x * 16 + lax.div(z, 8) * 8 + y_core, lax.rem(z, 8))


def kernel(
    src_ref, rcv_ref, pair_ref, freq_ref, out_ref,
    w_own, w_got, blocks, slices_a, slices_b, slices_c, picked, mates, terms, right_in, left_in,
    z_send, z_recv, w_send, w_recv, spread_send, spread_recv, back_send, back_recv,
    ring_send, ring_recv,
):
    p, f = lax.axis_index("pts"), lax.axis_index("freq")
    x, zh, yc = lax.div(p, 16), lax.rem(lax.div(p, 8), 2), lax.rem(p, 8)
    z = zh * 8 + f
    me = x * 8 + yc
    slices = (slices_a, slices_b, slices_c)

    def peer(t):
        return (lax.div(t, 8) * 16 + zh * 8 + lax.rem(t, 8), f)

    up, down = device(x, yc, lax.rem(z + 1, 16)), device(x, yc, lax.rem(z + 15, 16))
    barrier = pltpu.get_barrier_semaphore()
    for dz in (4, 12, 1, 15):
        pl.semaphore_signal(
            barrier, inc=1, device_id=device(x, yc, lax.rem(z + dz, 16)), device_id_type=MESH
        )

    @pl.loop(1, PEERS)
    def _(i):
        pl.semaphore_signal(
            barrier, inc=1, device_id=peer(lax.rem(me + i, PEERS)), device_id_type=MESH
        )

    for slot in range(3):
        scaled = (freq_ref[slot].astype(jnp.float32) + 1.0) / FBINS
        scaled = scaled * scaled
        w_own[slot] = jnp.full(w_own.shape[1:], scaled * scaled, jnp.float32)
    pl.semaphore_wait(barrier, PEERS - 1 + 4)

    far = lax.rem(f + 4, 8)

    def meeting(way):
        return (x * 16 + lax.rem(lax.div(f, 4) + way, 2) * 8 + yc, far)

    for number, (place, first, cols) in enumerate(CHUNKS):
        columns = pl.ds(first, cols)
        for slot, way in ((2, lax.rem(f, 2)),) if place else ((0, 0), (1, 1)):
            target = meeting(way)
            if first == 0:
                pltpu.make_async_remote_copy(
                    w_own.at[slot], w_got.at[place, zh], w_send, w_recv.at[place],
                    device_id=target, device_id_type=MESH,
                ).start()
            for side, ref in enumerate((src_ref, rcv_ref)):
                pltpu.make_async_remote_copy(
                    ref.at[slot, :, columns],
                    blocks.at[place, zh, pl.ds(256 * side, 256), columns],
                    z_send.at[side], z_recv.at[number],
                    device_id=target, device_id_type=MESH,
                ).start()

    terms[...] = jnp.zeros_like(terms)
    home = lax.div(far, 4)
    two = lax.rem(zh + home, 2) == lax.rem(f, 2)

    def arrived(ref, sem):
        pltpu.make_async_copy(ref, ref, sem).wait()

    def spread(number):
        place, first, cols = CHUNKS[number]
        columns = pl.ds(first, cols)
        arrived(blocks.at[place, :, :, columns], z_recv.at[number])

        @pl.loop(1, PEERS)
        def _(i):
            t = lax.rem(me + i, PEERS)
            pltpu.make_async_remote_copy(
                blocks.at[place, :, pl.ds(t * SLICE, SLICE), columns],
                slices[number].at[x, :, yc],
                spread_send.at[number], spread_recv.at[number],
                device_id=peer(t), device_id_type=MESH,
            ).start()

        pltpu.make_async_copy(
            blocks.at[place, :, pl.ds(me * SLICE, SLICE), columns],
            slices[number].at[x, :, yc],
            spread_recv.at[number],
        ).start()

    def back(number):
        place, first, cols = CHUNKS[number]
        columns = pl.ds(first, cols)
        arrived(slices[number], spread_recv.at[number])

        def pick(t):
            for r in range(ROUNDS):
                for h in range(2):
                    m = pair_ref[r, lax.div(t, 8) * 16 + h * 8 + lax.rem(t, 8)]
                    picked[place, t, r, h, :, columns] = slices[number][
                        lax.div(m, 16), lax.rem(lax.div(m, 8), 2), lax.rem(m, 8)
                    ]

        @pl.loop(1, PEERS)
        def _(i):
            t = lax.rem(me + i, PEERS)
            pick(t)
            pltpu.make_async_remote_copy(
                picked.at[place, t, :, :, :, columns],
                mates.at[place, :, :, pl.ds(me * SLICE, SLICE), columns],
                back_send.at[number], back_recv.at[number],
                device_id=peer(t), device_id_type=MESH,
            ).start()

        pick(me)
        pltpu.make_async_copy(
            picked.at[place, me, :, :, :, columns],
            mates.at[place, :, :, pl.ds(me * SLICE, SLICE), columns],
            back_recv.at[number],
        ).start()

    def gram(left, right):
        turned = jnp.concatenate([right[128:], -right[:128]], axis=0)
        both = jnp.concatenate([right, turned], axis=1)
        prod = lax.dot_general(
            left, both, (((0,), (0,)), ((), ())), preferred_element_type=jnp.float32
        )
        return prod[:, : right.shape[1]], prod[:, right.shape[1] :]

    def multiply(number):
        place, first, cols = CHUNKS[number]
        columns = pl.ds(first, cols)
        arrived(mates.at[place, :, :, :, columns], back_recv.at[number])
        weight = w_got[place, 0, 0:1, 0:1]

        @pl.loop(0, 2 * ROUNDS)
        def _(i):
            h, r = lax.div(i, ROUNDS), lax.rem(i, ROUNDS)
            src_re, src_im = gram(
                blocks[place, h, pl.ds(0, 256), :], mates[place, r, h, pl.ds(0, 256), columns]
            )
            rcv_re, rcv_im = gram(
                blocks[place, h, pl.ds(256, 256), :], mates[place, r, h, pl.ds(256, 256), columns]
            )
            term = weight * (src_re * rcv_re - src_im * rcv_im)
            terms[pl.ds(h * 8, 8), r, :, columns] += term.reshape(8, 32, cols)

    def finish(number):
        place, first, cols = CHUNKS[number]
        columns = pl.ds(first, cols)
        arrived(blocks.at[place, :, pl.ds(0, 31 * SLICE), columns], spread_send.at[number])
        arrived(picked.at[place, pl.ds(0, 31), :, :, :, columns], back_send.at[number])

    @pl.when(two)
    def _():
        arrived(w_got.at[1], w_recv.at[1])
        spread(0)
        back(0)

    arrived(w_got.at[0], w_recv.at[0])
    spread(1)
    back(1)

    @pl.when(two)
    def _():
        multiply(0)

    spread(2)
    back(2)
    multiply(1)
    multiply(2)

    def up_copy(step, r, source):
        return pltpu.make_async_remote_copy(
            source, right_in.at[step, r], ring_send.at[0, step, r], ring_recv.at[0, step, r],
            device_id=up, device_id_type=MESH,
        )

    def down_copy(step, r, source):
        return pltpu.make_async_remote_copy(
            source, left_in.at[step, r], ring_send.at[1, step, r], ring_recv.at[1, step, r],
            device_id=down, device_id_type=MESH,
        )

    for r in range(ROUNDS):
        up_copy(0, r, terms.at[lax.rem(z + 8, 16), r]).start()
        down_copy(0, r, terms.at[lax.rem(z + 9, 16), r]).start()

    @pl.loop(0, 6)
    def _(s):
        for r in range(ROUNDS):
            up_copy(s, r, right_in.at[s, r]).wait_recv()
            right_in[s, r] += terms[lax.rem(z + 7 - s, 16), r]
            up_copy(s + 1, r, right_in.at[s, r]).start()
            down_copy(s, r, left_in.at[s, r]).wait_recv()
            left_in[s, r] += terms[lax.rem(z + 10 + s, 16), r]
            down_copy(s + 1, r, left_in.at[s, r]).start()

    for r in range(ROUNDS):
        up_copy(6, r, right_in.at[6, r]).wait_recv()
        right_in[6, r] += terms[lax.rem(z + 1, 16), r]
        up_copy(7, r, right_in.at[6, r]).start()
    for r in range(ROUNDS):
        down_copy(6, r, left_in.at[6, r]).wait_recv()
        left_in[6, r] += terms[z, r]
        up_copy(7, r, right_in.at[7, r]).wait_recv()
        out_ref[r] = left_in[6, r] + right_in[7, r]

    @pl.when(two)
    def _():
        finish(0)

    finish(1)
    finish(2)
    arrived(src_ref, z_send.at[0])
    arrived(rcv_ref, z_send.at[1])
    arrived(w_own, w_send)

    @pl.loop(0, 7)
    def _(s):
        for r in range(ROUNDS):
            up_copy(s, r, right_in.at[s, r]).wait_send()
            down_copy(s, r, left_in.at[s, r]).wait_send()

    for r in range(ROUNDS):
        up_copy(7, r, right_in.at[6, r]).wait_send()


def on_device(green_src, green_rcv, pairing, freq_index):
    bf16, f32 = jnp.bfloat16, jnp.float32
    n = len(CHUNKS)
    dma = pltpu.SemaphoreType.DMA
    result = pl.pallas_call(
        kernel,
        out_shape=jax.ShapeDtypeStruct((ROUNDS, 32, 256), f32),
        in_specs=[
            pl.BlockSpec(memory_space=pl.ANY),
            pl.BlockSpec(memory_space=pl.ANY),
            pl.BlockSpec(memory_space=pltpu.SMEM),
            pl.BlockSpec(memory_space=pltpu.SMEM),
        ],
        out_specs=pl.BlockSpec(memory_space=pltpu.VMEM),
        scratch_shapes=[
            pltpu.VMEM((3, 8, 128), f32),
            pltpu.VMEM((2, 2, 8, 128), f32),
            pltpu.VMEM((2, 2, 512, 256), bf16),
            *(pltpu.VMEM((4, 2, 8, SLICE, cols), bf16) for _, _, cols in CHUNKS),
            pltpu.VMEM((2, PEERS, ROUNDS, 2, SLICE, 256), bf16),
            pltpu.VMEM((2, ROUNDS, 2, 512, 256), bf16),
            pltpu.VMEM((16, ROUNDS, 32, 256), f32),
            pltpu.VMEM((8, ROUNDS, 32, 256), f32),
            pltpu.VMEM((7, ROUNDS, 32, 256), f32),
            dma((2,)), dma((n,)), dma, dma((2,)),
            dma((n,)), dma((n,)), dma((n,)), dma((n,)),
            dma((2, 8, ROUNDS)), dma((2, 8, ROUNDS)),
        ],
        compiler_params=pltpu.CompilerParams(
            collective_id=0, has_side_effects=True, vmem_limit_bytes=48 << 20
        ),
    )(green_src.reshape(3, 256, 256), green_rcv.reshape(3, 256, 256), pairing, freq_index)
    return result.swapaxes(0, 1)


def solution(mesh):
    in_specs = (P("freq", None, None, "pts"), P("freq", None, None, "pts"), P(), P("freq"))
    out_specs = P(("pts", "freq"), None, None)
    return jax.shard_map(
        on_device, mesh=mesh, in_specs=in_specs, out_specs=out_specs, check_vma=False
    )
```

time: 326 us -> 131 us (0.40)
  waiting for transfers between devices: 215 us -> 0 us
  Pallas kernels: 0 us -> 126 us
  starting transfers between devices: 59.2 us -> 0 us
  local copies, waits for them, and re-layouts: 24.3 us -> 3.35 us
  between operations: 13.9 us -> 0.01 us
  other arithmetic: 8.6 us -> 0 us
    unnamed x4 -> x0, waiting for transfers between devices: 128 us -> none
    pallas_call x0 -> x1, Pallas kernels: none -> 126 us  [on_device(): pl.pallas_call(kernel, out_shape=jax.ShapeDtypeStruct((ROUNDS, 32, 256),...]
    all_to_all x6 -> x0, waiting for transfers between devices: 87.6 us -> none  [the longest x2 27.6 us: on_device(): lax.all_to_all(picked_r, 'pts', split_axis=0, concat_axis=3, tiled=True)]
    all_to_all x6 -> x0, starting transfers between devices: 59.1 us -> none  [the longest x1 21 us: on_device(): lax.all_to_all(green_src[None], 'pts', split_axis=3, concat_axis=0, tiled...]
    unnamed x42 -> x8, local copies, waits for them, and re-layouts: 11.1 us -> 2.67 us
    gather x4 -> x0, local copies, waits for them, and re-layouts: 5.44 us -> none  [the longest x2 2.72 us: on_device(): picked_r = jnp.take(spread_r, pairing[step], axis=0)]
    add x2 -> x0, other arithmetic: 4.82 us -> none  [partial_rows(): total + weights[freq_slot] * (prod_s[:, :cols] * prod_r[:, :cols] - prod_...]
    slice x7 -> x0, local copies, waits for them, and re-layouts: 3.59 us -> none  [the longest x4 2.19 us: right_side(): first = jnp.concatenate([block[:, 0], block[:, 1]], axis=1)]
  transfers between devices with their start and end apart: 8 -> 0, of which waited for: 8 -> 0; matrix products, arithmetic and copies ran while one was open for 7% -> 0% of each run, Pallas kernels for 0% -> 0%
where the time goes in v1:
time: 131 us; the launch traced here: 130 us
  Pallas kernels  126 us (96%)
  local copies, waits for them, and re-layouts  3.35 us (3%)
    pallas_call x1, Pallas kernels, on_device(): pl.pallas_call(kernel, out_shape=jax.ShapeDtypeStruct((ROUNDS, 32, 256),...  126 us
    unnamed x8, local copies, waits for them, and re-layouts  2.67 us

profile of v1, /device:TPU:24, one launch (start us, length us, event | category | flops | bytes accessed | tf_op | source)
XLA Modules:
  0.0 129.6 jit_solution(7127916879435305111)
XLA Ops:
  0.0 0.0 copy-start.2
  0.0 0.0 copy-start.3
  0.0 0.7 copy-done.2
  0.7 0.0 copy-done.3
  0.7 0.0 copy-start
  0.7 1.0 copy-done
  1.7 0.0 copy-start.1
  1.7 1.0 copy-done.1
  2.7 126.2 %shard_map.46 = f32[2,32,256]{2,1,0:T(8,128)S(1)} custom-call(bf16[3,256,256]{2,1,0:T(8,128)(2,1)S(1)} %bitcast.3, bf16[3,256,256]{2,1,0:T(8,128)(2,1)S(1)} %bitcast.4, s32[2,64]{1,0:T(2,128)S(1)} %copy-done.2, s32[3]{0:T(128)S(1)} %copy-done.3), custom_call_target="tpu_custom_call" | custom-call | tf_op jit(solution)/shard_map/pallas_call | solution.py:248
  128.9 0.7 copy.5
Async XLA Ops:
  0.0 0.7 copy-start.2
  0.0 0.7 copy-start.3
  0.7 1.0 copy-start
  1.7 1.0 copy-start.1

commit v2 on v1

v2 whole, which is shorter than its diff:
```python
import functools

import jax
import jax.numpy as jnp
from jax import lax
from jax.experimental import pallas as pl
from jax.experimental.pallas import tpu as pltpu
from jax.sharding import PartitionSpec as P

ROUNDS = 2
FBINS = 64
PEERS = 32
SLICE = 16
MESH = pl.DeviceIdType.MESH
CHUNKS = ((1, 0), (0, 0), (1, 128), (0, 128))
COLS = 128


def device(x, y_core, z):
    return (x * 16 + lax.div(z, 8) * 8 + y_core, lax.rem(z, 8))


def kernel(src_ref, rcv_ref, pair_ref, freq_ref, out_ref, *scratch):
    n = len(CHUNKS)
    blocks, slices, picked, mates = (scratch[i * n : (i + 1) * n] for i in range(4))
    (
        w_own, w_got, terms, up_in, down_in,
        z_send, z_recv, w_send, w_recv, spread_send, spread_recv, back_send, back_recv,
        ring_send, ring_recv,
    ) = scratch[4 * n :]
    p, f = lax.axis_index("pts"), lax.axis_index("freq")
    x, zh, yc = lax.div(p, 16), lax.rem(lax.div(p, 8), 2), lax.rem(p, 8)
    z = zh * 8 + f
    me = x * 8 + yc

    def peer(t):
        return (lax.div(t, 8) * 16 + zh * 8 + lax.rem(t, 8), f)

    up, down = device(x, yc, lax.rem(z + 1, 16)), device(x, yc, lax.rem(z + 15, 16))
    barrier = pltpu.get_barrier_semaphore()
    for dz in (4, 12, 1, 15):
        pl.semaphore_signal(
            barrier, inc=1, device_id=device(x, yc, lax.rem(z + dz, 16)), device_id_type=MESH
        )

    @pl.loop(1, PEERS)
    def _(i):
        pl.semaphore_signal(
            barrier, inc=1, device_id=peer(lax.rem(me + i, PEERS)), device_id_type=MESH
        )

    for slot in range(3):
        scaled = (freq_ref[slot].astype(jnp.float32) + 1.0) / FBINS
        scaled = scaled * scaled
        w_own[slot] = jnp.full(w_own.shape[1:], scaled * scaled, jnp.float32)
    pl.semaphore_wait(barrier, PEERS - 1 + 4)

    far = lax.rem(f + 4, 8)

    def meeting(way):
        return (x * 16 + lax.rem(lax.div(f, 4) + way, 2) * 8 + yc, far)

    def arrived(ref, sem):
        pltpu.make_async_copy(ref, ref, sem).wait()

    def z_step(number, k):
        place, first = CHUNKS[number]
        slot, row = (2, k) if place else (lax.rem(k, 2), lax.div(k, 2))
        target = meeting(lax.rem(f, 2) if place else slot)
        for side, ref in enumerate((src_ref, rcv_ref)):
            pltpu.make_async_remote_copy(
                ref.at[slot, row, :, pl.ds(first, COLS)],
                blocks[number].at[16 * side + row, zh],
                z_send.at[number, side], z_recv.at[number],
                device_id=target, device_id_type=MESH,
            ).start()

    def z_steps(number, start, count):
        @pl.loop(start, start + count)
        def _(k):
            z_step(number, k)

    def z_between(i, plan):
        for number, start, count in plan:
            before = lax.div((i - 1) * count, PEERS - 1)

            @pl.when(lax.div(i * count, PEERS - 1) > before)
            def _(number=number, k=start + before):
                z_step(number, k)

    def launched(number):
        place, first = CHUNKS[number]
        slots = pl.ds(2, 1) if place else pl.ds(0, 2)
        for side, ref in enumerate((src_ref, rcv_ref)):
            arrived(ref.at[slots, :, :, pl.ds(first, COLS)], z_send.at[number, side])

    for slot, place, way in ((2, 1, lax.rem(f, 2)), (0, 0, 0), (1, 0, 1)):
        pltpu.make_async_remote_copy(
            w_own.at[slot], w_got.at[place, zh], w_send, w_recv.at[place],
            device_id=meeting(way), device_id_type=MESH,
        ).start()
    z_steps(0, 0, 16)
    z_steps(1, 0, 8)
    terms[...] = jnp.zeros_like(terms)
    two = lax.rem(zh + lax.div(far, 4), 2) == lax.rem(f, 2)

    def spread(number, plan=()):
        arrived(blocks[number], z_recv.at[number])

        @pl.loop(1, PEERS)
        def _(i):
            z_between(i, plan)
            t = lax.rem(me + i, PEERS)
            pltpu.make_async_remote_copy(
                blocks[number].at[t], slices[number].at[x, yc],
                spread_send.at[number], spread_recv.at[number],
                device_id=peer(t), device_id_type=MESH,
            ).start()

        pltpu.make_async_copy(
            blocks[number].at[me], slices[number].at[x, yc], spread_recv.at[number]
        ).start()

    def back(number, plan=()):
        arrived(slices[number], spread_recv.at[number])

        def pick(t):
            for r in range(ROUNDS):
                for h in range(2):
                    m = pair_ref[r, lax.div(t, 8) * 16 + h * 8 + lax.rem(t, 8)]
                    picked[number][t, r, h] = slices[number][
                        lax.div(m, 16), lax.rem(m, 8), lax.rem(lax.div(m, 8), 2)
                    ]

        @pl.loop(1, PEERS)
        def _(i):
            z_between(i, plan)
            t = lax.rem(me + i, PEERS)
            pick(t)
            pltpu.make_async_remote_copy(
                picked[number].at[t], mates[number].at[me],
                back_send.at[number], back_recv.at[number],
                device_id=peer(t), device_id_type=MESH,
            ).start()

        pick(me)
        pltpu.make_async_copy(
            picked[number].at[me], mates[number].at[me], back_recv.at[number]
        ).start()

    def gram(left, right):
        turned = jnp.concatenate([right[128:], -right[:128]], axis=0)
        both = jnp.concatenate([right, turned], axis=1)
        prod = lax.dot_general(
            left, both, (((0,), (0,)), ((), ())), preferred_element_type=jnp.float32
        )
        return prod[:, : right.shape[1]], prod[:, right.shape[1] :]

    def multiply(number):
        place, first = CHUNKS[number]
        half = first // COLS
        arrived(mates[number], back_recv.at[number])
        weight = w_got[place, 0, 0:1, 0:1]

        def own(h, side):
            parts = [
                blocks[k][pl.ds(16 * side, 16), h].reshape(256, COLS)
                for k in range(n)
                if CHUNKS[k][0] == place
            ]
            return jnp.concatenate(parts, axis=1)

        @pl.loop(0, 2 * ROUNDS)
        def _(i):
            h, r = lax.div(i, ROUNDS), lax.rem(i, ROUNDS)
            src_re, src_im = gram(
                own(h, 0), mates[number][pl.ds(0, 16), r, h].reshape(256, COLS)
            )
            rcv_re, rcv_im = gram(
                own(h, 1), mates[number][pl.ds(16, 16), r, h].reshape(256, COLS)
            )
            term = weight * (src_re * rcv_re - src_im * rcv_im)
            terms[half, pl.ds(h * 8, 8), r] += term.reshape(8, 32, COLS)

    def finish(number):
        arrived(blocks[number].at[pl.ds(0, PEERS - 1)], spread_send.at[number])
        arrived(picked[number].at[pl.ds(0, PEERS - 1)], back_send.at[number])

    def up_copy(half, step, source):
        return pltpu.make_async_remote_copy(
            source, up_in.at[half, step], ring_send.at[0, half, step],
            ring_recv.at[0, half, step], device_id=up, device_id_type=MESH,
        )

    def down_copy(half, step, source):
        return pltpu.make_async_remote_copy(
            source, down_in.at[half, step], ring_send.at[1, half, step],
            ring_recv.at[1, half, step], device_id=down, device_id_type=MESH,
        )

    def ring_start(half):
        up_copy(half, 0, terms.at[half, lax.rem(z + 8, 16)]).start()
        down_copy(half, 0, terms.at[half, lax.rem(z + 9, 16)]).start()

    def ring_step(half, s):
        up_copy(half, s, up_in.at[half, s]).wait_recv()
        up_in[half, s] += terms[half, lax.rem(z + 7 - s, 16)]
        up_copy(half, s + 1, up_in.at[half, s]).start()
        down_copy(half, s, down_in.at[half, s]).wait_recv()
        down_in[half, s] += terms[half, lax.rem(z + 10 + s, 16)]
        if not isinstance(s, int) or s < 6:
            down_copy(half, s + 1, down_in.at[half, s]).start()

    def ring_end(half):
        up_copy(half, 7, up_in.at[half, 7]).wait_recv()
        out_ref[:, :, half * COLS : (half + 1) * COLS] = up_in[half, 7] + down_in[half, 6]

    @pl.when(two)
    def _():
        arrived(w_got.at[1], w_recv.at[1])
        spread(0, ((1, 8, 10),))
        z_steps(1, 18, 6)
        back(0, ((1, 24, 8), (2, 0, 8)))

    @pl.when(jnp.logical_not(two))
    def _():
        z_steps(1, 8, 24)
        z_steps(2, 0, 8)

    arrived(w_got.at[0], w_recv.at[0])
    spread(1, ((2, 8, 8),))
    z_steps(3, 0, 6)
    back(1, ((3, 6, 16),))

    @pl.when(two)
    def _():
        spread(2, ((3, 22, 10),))
        back(2)

    @pl.when(jnp.logical_not(two))
    def _():
        z_steps(3, 22, 10)

    spread(3)

    @pl.when(two)
    def _():
        multiply(0)

    multiply(1)
    ring_start(0)
    back(3)
    ring_step(0, 0)
    ring_step(0, 1)

    @pl.when(two)
    def _():
        multiply(2)

    multiply(3)
    ring_start(1)
    ring_step(0, 2)
    ring_step(1, 0)
    ring_step(0, 3)
    ring_step(1, 1)
    ring_step(0, 4)
    ring_step(1, 2)
    ring_step(0, 5)
    ring_step(1, 3)
    ring_step(0, 6)
    ring_step(1, 4)
    ring_step(1, 5)
    ring_step(1, 6)
    ring_end(0)
    ring_end(1)

    @pl.when(two)
    def _():
        finish(0)
        finish(2)

    finish(1)
    finish(3)
    for number in range(n):
        launched(number)
    arrived(w_own, w_send)

    for half in range(2):
        for step in range(8):
            up_copy(half, step, up_in.at[half, step]).wait_send()
        for step in range(7):
            down_copy(half, step, down_in.at[half, step]).wait_send()


def on_device(green_src, green_rcv, pairing, freq_index):
    bf16, f32 = jnp.bfloat16, jnp.float32
    n = len(CHUNKS)
    dma = pltpu.SemaphoreType.DMA
    result = pl.pallas_call(
        kernel,
        out_shape=jax.ShapeDtypeStruct((ROUNDS, 32, 256), f32),
        in_specs=[
            pl.BlockSpec(memory_space=pl.ANY),
            pl.BlockSpec(memory_space=pl.ANY),
            pl.BlockSpec(memory_space=pltpu.SMEM),
            pl.BlockSpec(memory_space=pltpu.SMEM),
        ],
        out_specs=pl.BlockSpec(memory_space=pltpu.VMEM),
        scratch_shapes=[
            *(pltpu.VMEM((PEERS, 2, SLICE, COLS), bf16) for _ in CHUNKS),
            *(pltpu.VMEM((4, 8, 2, SLICE, COLS), bf16) for _ in CHUNKS),
            *(pltpu.VMEM((PEERS, ROUNDS, 2, SLICE, COLS), bf16) for _ in CHUNKS),
            *(pltpu.VMEM((PEERS, ROUNDS, 2, SLICE, COLS), bf16) for _ in CHUNKS),
            pltpu.VMEM((3, 8, 128), f32),
            pltpu.VMEM((2, 2, 8, 128), f32),
            pltpu.VMEM((2, 16, ROUNDS, 32, COLS), f32),
            pltpu.VMEM((2, 8, ROUNDS, 32, COLS), f32),
            pltpu.VMEM((2, 7, ROUNDS, 32, COLS), f32),
            dma((n, 2)), dma((n,)), dma, dma((2,)),
            dma((n,)), dma((n,)), dma((n,)), dma((n,)),
            dma((2, 2, 8)), dma((2, 2, 8)),
        ],
        compiler_params=pltpu.CompilerParams(
            collective_id=0, has_side_effects=True, vmem_limit_bytes=60 << 20
        ),
    )(
        green_src.reshape(3, 16, 16, 256), green_rcv.reshape(3, 16, 16, 256),
        pairing, freq_index,
    )
    return result.swapaxes(0, 1)


def solution(mesh):
    in_specs = (P("freq", None, None, "pts"), P("freq", None, None, "pts"), P(), P("freq"))
    out_specs = P(("pts", "freq"), None, None)
    return jax.shard_map(
        on_device, mesh=mesh, in_specs=in_specs, out_specs=out_specs, check_vma=False
    )
```

time: 131 us -> 115 us (0.88); the launches traced: 130 us -> 115 us
  Pallas kernels: 126 us -> 114 us
  local copies, waits for them, and re-layouts: 3.35 us -> 1.52 us
    pallas_call x1, Pallas kernels: 126 us -> 114 us  [on_device(): pl.pallas_call(kernel, out_shape=jax.ShapeDtypeStruct((ROUNDS, 32, 256),...]
    unnamed x8 -> x0, local copies, waits for them, and re-layouts: 2.67 us -> none
where the time goes in v2:
time: 115 us
  Pallas kernels  114 us (99%)
  local copies, waits for them, and re-layouts  1.52 us (1%)
    pallas_call x1, Pallas kernels, on_device(): pl.pallas_call(kernel, out_shape=jax.ShapeDtypeStruct((ROUNDS, 32, 256),...  114 us

profile of v2, /device:TPU:24, one launch (start us, length us, event | category | flops | bytes accessed | tf_op | source)
XLA Modules:
  0.0 115.1 jit_solution(15178005099589303797)
XLA Ops:
  0.0 113.6 %shard_map.46 = f32[2,32,256]{2,1,0:T(8,128)} custom-call(bf16[3,16,16,256]{3,2,1,0:T(8,128)(2,1)} %bitcast.3, bf16[3,16,16,256]{3,2,1,0:T(8,128)(2,1)} %bitcast.4, s32[2,64]{1,0:T(2,128)} %pair_ref.1, s32[3]{0:T(128)} %freq_ref.1), custom_call_target="tpu_custom_call" | custom-call | tf_op jit(solution)/shard_map/pallas_call | solution.py:299
  113.6 1.5 %copy.5 = f32[32,2,256]{2,1,0:T(2,128)} copy(f32[32,2,256]{2,0,1:T(8,128)} %bitcast.5) | data formatting | bytes 131072 | tf_op jit(solution)/shard_map/transpose | solution.py:330

commit v3 on v2

v3 whole, which is shorter than its diff:
```python
import functools

import jax
import jax.numpy as jnp
from jax import lax
from jax.experimental import pallas as pl
from jax.experimental.pallas import tpu as pltpu
from jax.sharding import PartitionSpec as P

ROUNDS = 2
FBINS = 64
PEERS = 32
SLICE = 16
MESH = pl.DeviceIdType.MESH
PLACES = (1, 0, 0, 1)
SPREAD = 3
COLS = 128
GATHER = (
    (8, 2), (7, 1), (5, -1), (-5, 1), (-7, -1),
    (4, 2), (3, 1), (-3, -1), (-4, -2), (1, 1), (-1, -1),
)
LEADERS = (6, -6, 2, -2)
NEIGHBOURS = (-6, -4, -2, -1, 1, 2, 4, 6)


def device(x, y_core, z):
    return (x * 16 + lax.div(z, 8) * 8 + y_core, lax.rem(z, 8))


def kernel(src_ref, rcv_ref, pair_ref, freq_ref, out_ref, *scratch):
    n = len(PLACES)
    blocks = scratch[:n]
    slices, picked, mates = (scratch[n + i * SPREAD : n + (i + 1) * SPREAD] for i in range(3))
    (
        w_own, w_got, terms, near, led, last,
        z_send, z_recv, w_send, w_recv, spread_send, spread_recv, back_send, back_recv,
        near_send, near_recv, last_send, last_recv,
    ) = scratch[n + 3 * SPREAD :]
    p, f = lax.axis_index("pts"), lax.axis_index("freq")
    x, zh, yc = lax.div(p, 16), lax.rem(lax.div(p, 8), 2), lax.rem(p, 8)
    z = zh * 8 + f
    me = x * 8 + yc

    def peer(t):
        return (lax.div(t, 8) * 16 + zh * 8 + lax.rem(t, 8), f)

    def plane(shift):
        return lax.rem(z + (shift + 16), 16)

    barrier = pltpu.get_barrier_semaphore()
    for shift in NEIGHBOURS:
        pl.semaphore_signal(
            barrier, inc=1, device_id=device(x, yc, plane(shift)), device_id_type=MESH
        )

    @pl.loop(1, PEERS)
    def _(i):
        pl.semaphore_signal(
            barrier, inc=1, device_id=peer(lax.rem(me + i, PEERS)), device_id_type=MESH
        )

    for slot in range(3):
        scaled = (freq_ref[slot].astype(jnp.float32) + 1.0) / FBINS
        scaled = scaled * scaled
        w_own[slot] = jnp.full(w_own.shape[1:], scaled * scaled, jnp.float32)
    pl.semaphore_wait(barrier, PEERS - 1 + len(NEIGHBOURS))

    far = lax.rem(f + 4, 8)

    def meeting(way):
        return (x * 16 + lax.rem(lax.div(f, 4) + way, 2) * 8 + yc, far)

    def arrived(ref, sem):
        pltpu.make_async_copy(ref, ref, sem).wait()

    def z_step(number, k):
        way, row = lax.rem(k, 2), lax.div(k, 2)
        if PLACES[number]:
            slot, half = 2, way if number == 0 else 1 - way
        else:
            slot, half = way, number - 1
        for side, ref in enumerate((src_ref, rcv_ref)):
            pltpu.make_async_remote_copy(
                ref.at[slot, row, :, pl.ds(pl.multiple_of(half * COLS, COLS), COLS)],
                blocks[number].at[16 * side + row, zh],
                z_send.at[number, side], z_recv.at[number],
                device_id=meeting(way), device_id_type=MESH,
            ).start()

    def z_steps(number, start, count):
        @pl.loop(start, start + count)
        def _(k):
            z_step(number, k)

    def z_between(i, plan):
        for number, start, count in plan:
            before = lax.div((i - 1) * count, PEERS - 1)

            @pl.when(lax.div(i * count, PEERS - 1) > before)
            def _(number=number, k=start + before):
                z_step(number, k)

    def launched(number):
        for side, ref in enumerate((src_ref, rcv_ref)):
            if PLACES[number]:
                arrived(ref.at[pl.ds(2, 1)], z_send.at[number, side])
            else:
                arrived(
                    ref.at[pl.ds(0, 2), :, :, pl.ds((number - 1) * COLS, COLS)],
                    z_send.at[number, side],
                )

    for way in range(2):
        for slot, place in ((2, 1), (way, 0)):
            pltpu.make_async_remote_copy(
                w_own.at[slot], w_got.at[place, zh], w_send.at[place], w_recv.at[place],
                device_id=meeting(way), device_id_type=MESH,
            ).start()
    z_steps(0, 0, 32)
    z_steps(1, 0, 20)
    terms[...] = jnp.zeros_like(terms)
    mine = lax.rem(zh + lax.div(far, 4), 2)

    def spread(number, plan=()):
        arrived(blocks[number], z_recv.at[number])

        @pl.loop(1, PEERS)
        def _(i):
            z_between(i, plan)
            t = lax.rem(me + i * 13, PEERS)
            pltpu.make_async_remote_copy(
                blocks[number].at[t], slices[number].at[x, yc],
                spread_send.at[number], spread_recv.at[number],
                device_id=peer(t), device_id_type=MESH,
            ).start()

        pltpu.make_async_copy(
            blocks[number].at[me], slices[number].at[x, yc], spread_recv.at[number]
        ).start()

    def back(number, plan=()):
        arrived(slices[number], spread_recv.at[number])

        def pick(t):
            for r in range(ROUNDS):
                for h in range(2):
                    m = pair_ref[r, lax.div(t, 8) * 16 + h * 8 + lax.rem(t, 8)]
                    picked[number][t, r, h] = slices[number][
                        lax.div(m, 16), lax.rem(m, 8), lax.rem(lax.div(m, 8), 2)
                    ]

        @pl.loop(1, PEERS)
        def _(i):
            z_between(i, plan)
            t = lax.rem(me + i * 13, PEERS)
            pick(t)
            pltpu.make_async_remote_copy(
                picked[number].at[t], mates[number].at[me],
                back_send.at[number], back_recv.at[number],
                device_id=peer(t), device_id_type=MESH,
            ).start()

        pick(me)
        pltpu.make_async_copy(
            picked[number].at[me], mates[number].at[me], back_recv.at[number]
        ).start()

    def gram(left, right):
        turned = jnp.concatenate([right[128:], -right[:128]], axis=0)
        both = jnp.concatenate([right, turned], axis=1)
        prod = lax.dot_general(
            left, both, (((0,), (0,)), ((), ())), preferred_element_type=jnp.float32
        )
        return prod[:, : right.shape[1]], prod[:, right.shape[1] :]

    def multiply(number):
        arrived(mates[number], back_recv.at[number])
        place = PLACES[number]
        weight = w_got[place, 0, 0:1, 0:1]
        pair = (0, 3) if place else (1, 2)
        first = mine if place else 0
        half = mine if place else number - 1

        def own(h, side):
            parts = [blocks[k][pl.ds(16 * side, 16), h].reshape(256, COLS) for k in pair]
            return jnp.concatenate(parts, axis=1)

        @pl.loop(0, 2 * ROUNDS)
        def _(i):
            h, r = lax.div(i, ROUNDS), lax.rem(i, ROUNDS)
            src_re, src_im = gram(
                own(h, 0), mates[number][pl.ds(0, 16), r, h].reshape(256, COLS)
            )
            rcv_re, rcv_im = gram(
                own(h, 1), mates[number][pl.ds(16, 16), r, h].reshape(256, COLS)
            )
            term = weight * (src_re * rcv_re - src_im * rcv_im)
            term = term.reshape(2, 4, 32, COLS)
            terms[half, pl.ds(h * 8 + 4 * first, 4), r] += term[0]
            terms[half, pl.ds(h * 8 + 4 * (1 - first), 4), r] += term[1]

    def finish(number):
        arrived(blocks[number].at[pl.ds(0, PEERS - 1)], spread_send.at[number])
        arrived(picked[number].at[pl.ds(0, PEERS - 1)], back_send.at[number])

    def gather_copy(half, i):
        dist, shift = GATHER[i]
        return pltpu.make_async_remote_copy(
            terms.at[half, plane(dist)], near.at[half, i],
            near_send.at[half, i], near_recv.at[half, i],
            device_id=device(x, yc, plane(shift)), device_id_type=MESH,
        )

    def lead_copy(half, i):
        return pltpu.make_async_remote_copy(
            led.at[half, i], last.at[half, i], last_send.at[half, i], last_recv.at[half, i],
            device_id=device(x, yc, plane(LEADERS[i])), device_id_type=MESH,
        )

    def gather(half):
        for i in range(len(GATHER)):
            gather_copy(half, i).start()

    def gathered(half, lead):
        total = terms[half, plane(lead)]
        for i, (dist, shift) in enumerate(GATHER):
            if dist - shift == lead:
                gather_copy(half, i).wait_recv()
                total = total + near[half, i]
        return total

    def lead(half):
        for i, dist in enumerate(LEADERS):
            led[half, i] = gathered(half, dist)
            lead_copy(half, i).start()

    def total(half):
        result = gathered(half, 0)
        for i in range(len(LEADERS)):
            lead_copy(half, i).wait_recv()
            result = result + last[half, i]
        out_ref[:, :, half * COLS : (half + 1) * COLS] = result

    for place in range(2):
        arrived(w_got.at[place], w_recv.at[place])
    spread(0, ((1, 20, 12), (2, 0, 2),))
    z_steps(2, 2, 8)
    back(0, ((2, 10, 22),))
    spread(1, ((3, 0, 12),))
    z_steps(3, 12, 6)
    back(1, ((3, 18, 14),))
    spread(2)
    multiply(1)
    back(2)
    arrived(blocks[3], z_recv.at[3])
    multiply(0)
    gather(0)
    lead(0)
    multiply(2)
    gather(1)
    lead(1)
    total(0)
    total(1)

    for number in range(SPREAD):
        finish(number)
    for number in range(n):
        launched(number)
    for place in range(2):
        arrived(w_own.at[pl.ds(0, 2)], w_send.at[place])

    for half in range(2):
        for i in range(len(GATHER)):
            gather_copy(half, i).wait_send()
        for i in range(len(LEADERS)):
            lead_copy(half, i).wait_send()


def on_device(green_src, green_rcv, pairing, freq_index):
    bf16, f32 = jnp.bfloat16, jnp.float32
    n = len(PLACES)
    dma = pltpu.SemaphoreType.DMA
    result = pl.pallas_call(
        kernel,
        out_shape=jax.ShapeDtypeStruct((ROUNDS, 32, 256), f32),
        in_specs=[
            pl.BlockSpec(memory_space=pl.ANY),
            pl.BlockSpec(memory_space=pl.ANY),
            pl.BlockSpec(memory_space=pltpu.SMEM),
            pl.BlockSpec(memory_space=pltpu.SMEM),
        ],
        out_specs=pl.BlockSpec(memory_space=pltpu.VMEM),
        scratch_shapes=[
            *(pltpu.VMEM((PEERS, 2, SLICE, COLS), bf16) for _ in PLACES),
            *(pltpu.VMEM((4, 8, 2, SLICE, COLS), bf16) for _ in range(SPREAD)),
            *(pltpu.VMEM((PEERS, ROUNDS, 2, SLICE, COLS), bf16) for _ in range(SPREAD)),
            *(pltpu.VMEM((PEERS, ROUNDS, 2, SLICE, COLS), bf16) for _ in range(SPREAD)),
            pltpu.VMEM((3, 8, 128), f32),
            pltpu.VMEM((2, 2, 8, 128), f32),
            pltpu.VMEM((2, 16, ROUNDS, 32, COLS), f32),
            pltpu.VMEM((2, len(GATHER), ROUNDS, 32, COLS), f32),
            pltpu.VMEM((2, len(LEADERS), ROUNDS, 32, COLS), f32),
            pltpu.VMEM((2, len(LEADERS), ROUNDS, 32, COLS), f32),
            dma((n, 2)), dma((n,)), dma((2,)), dma((2,)),
            dma((n,)), dma((n,)), dma((n,)), dma((n,)),
            dma((2, len(GATHER))), dma((2, len(GATHER))),
            dma((2, len(LEADERS))), dma((2, len(LEADERS))),
        ],
        compiler_params=pltpu.CompilerParams(
            collective_id=0, has_side_effects=True, vmem_limit_bytes=60 << 20
        ),
    )(
        green_src.reshape(3, 16, 16, 256), green_rcv.reshape(3, 16, 16, 256),
        pairing, freq_index,
    )
    return result.swapaxes(0, 1)


def solution(mesh):
    in_specs = (P("freq", None, None, "pts"), P("freq", None, None, "pts"), P(), P("freq"))
    out_specs = P(("pts", "freq"), None, None)
    return jax.shard_map(
        on_device, mesh=mesh, in_specs=in_specs, out_specs=out_specs, check_vma=False
    )
```

time: 115 us -> 100 us (0.87)
  the two profiles are of different devices: /device:TPU:24 before, /device:TPU:64 now
where the time goes in v3:
time: 100 us
  Pallas kernels  98.5 us (98%)
  local copies, waits for them, and re-layouts  1.52 us (2%)
    pallas_call x1, Pallas kernels, on_device(): pl.pallas_call(kernel, out_shape=jax.ShapeDtypeStruct((ROUNDS, 32, 256),...  98.5 us

profile of v3, /device:TPU:64, one launch (start us, length us, event | category | flops | bytes accessed | tf_op | source)
XLA Modules:
  0.0 100.0 jit_solution(6268009939242452548)
XLA Ops:
  0.0 98.5 %shard_map.46 = f32[2,32,256]{2,1,0:T(8,128)} custom-call(bf16[3,16,16,256]{3,2,1,0:T(8,128)(2,1)} %bitcast.3, bf16[3,16,16,256]{3,2,1,0:T(8,128)(2,1)} %bitcast.4, s32[2,64]{1,0:T(2,128)} %pair_ref.1, s32[3]{0:T(128)} %freq_ref.1), custom_call_target="tpu_custom_call" | custom-call | tf_op jit(solution)/shard_map/pallas_call | solution.py:283
  98.5 1.5 %copy.5 = f32[32,2,256]{2,1,0:T(2,128)} copy(f32[32,2,256]{2,0,1:T(8,128)} %bitcast.5) | data formatting | bytes 131072 | tf_op jit(solution)/shard_map/transpose | solution.py:316

commit v4 on v3

--- a/solution.py
+++ b/solution.py
@@ -13,6 +13,7 @@
 SLICE = 16
 MESH = pl.DeviceIdType.MESH
 PLACES = (1, 0, 0, 1)
+GROUP = 2
 SPREAD = 3
 COLS = 128
 GATHER = (
@@ -74,15 +75,16 @@
         pltpu.make_async_copy(ref, ref, sem).wait()
 
     def z_step(number, k):
-        way, row = lax.rem(k, 2), lax.div(k, 2)
+        way, row = lax.rem(k, 2), lax.div(k, 2) * GROUP
+        rows = pl.ds(row, GROUP)
         if PLACES[number]:
             slot, half = 2, way if number == 0 else 1 - way
         else:
             slot, half = way, number - 1
         for side, ref in enumerate((src_ref, rcv_ref)):
             pltpu.make_async_remote_copy(
-                ref.at[slot, row, :, pl.ds(pl.multiple_of(half * COLS, COLS), COLS)],
-                blocks[number].at[16 * side + row, zh],
+                ref.at[slot, rows, :, pl.ds(pl.multiple_of(half * COLS, COLS), COLS)],
+                blocks[number].at[pl.ds(16 * side + row, GROUP), zh],
                 z_send.at[number, side], z_recv.at[number],
                 device_id=meeting(way), device_id_type=MESH,
             ).start()
@@ -116,8 +118,8 @@
                 w_own.at[slot], w_got.at[place, zh], w_send.at[place], w_recv.at[place],
                 device_id=meeting(way), device_id_type=MESH,
             ).start()
-    z_steps(0, 0, 32)
-    z_steps(1, 0, 20)
+    z_steps(0, 0, 16)
+    z_steps(1, 0, 10)
     terms[...] = jnp.zeros_like(terms)
     mine = lax.rem(zh + lax.div(far, 4), 2)
 
@@ -243,18 +245,18 @@
 
     for place in range(2):
         arrived(w_got.at[place], w_recv.at[place])
-    spread(0, ((1, 20, 12), (2, 0, 2),))
-    z_steps(2, 2, 8)
-    back(0, ((2, 10, 22),))
-    spread(1, ((3, 0, 12),))
-    z_steps(3, 12, 6)
-    back(1, ((3, 18, 14),))
+    spread(0, ((1, 10, 6), (2, 0, 1),))
+    z_steps(2, 1, 4)
+    back(0, ((2, 5, 11),))
+    spread(1, ((3, 0, 6),))
+    z_steps(3, 6, 3)
+    back(1, ((3, 9, 7),))
     spread(2)
     multiply(1)
-    back(2)
     arrived(blocks[3], z_recv.at[3])
     multiply(0)
     gather(0)
+    back(2)
     lead(0)
     multiply(2)
     gather(1)

time: 100 us -> 97.1 us (0.971)
  the two profiles are of different devices: /device:TPU:64 before, /device:TPU:24 now
where the time goes in v4:
time: 97.1 us; the launch traced here: 96.1 us
  Pallas kernels  94.5 us (97%)
  local copies, waits for them, and re-layouts  1.52 us (2%)
    pallas_call x1, Pallas kernels, on_device(): pl.pallas_call(kernel, out_shape=jax.ShapeDtypeStruct((ROUNDS, 32, 256),...  94.5 us

profile of v4, /device:TPU:24, one launch (start us, length us, event | category | flops | bytes accessed | tf_op | source)
XLA Modules:
  0.0 96.1 jit_solution(1252620526175129740)
XLA Ops:
  0.0 94.5 %shard_map.46 = f32[2,32,256]{2,1,0:T(8,128)} custom-call(bf16[3,16,16,256]{3,2,1,0:T(8,128)(2,1)} %bitcast.3, bf16[3,16,16,256]{3,2,1,0:T(8,128)(2,1)} %bitcast.4, s32[2,64]{1,0:T(2,128)} %pair_ref.1, s32[3]{0:T(128)} %freq_ref.1), custom_call_target="tpu_custom_call" | custom-call | tf_op jit(solution)/shard_map/pallas_call | solution.py:285
  94.5 1.5 %copy.5 = f32[32,2,256]{2,1,0:T(2,128)} copy(f32[32,2,256]{2,0,1:T(8,128)} %bitcast.5) | data formatting | bytes 131072 | tf_op jit(solution)/shard_map/transpose | solution.py:318

commit v5 on v4

--- a/solution.py
+++ b/solution.py
@@ -257,9 +257,9 @@
     multiply(0)
     gather(0)
     back(2)
-    lead(0)
     multiply(2)
     gather(1)
+    lead(0)
     lead(1)
     total(0)
     total(1)

time: 97.1 us -> 102 us (1.050)
  the two profiles are of different devices: /device:TPU:24 before, /device:TPU:32 now
where the time goes in v5:
time: 102 us
  Pallas kernels  100 us (98%)
  local copies, waits for them, and re-layouts  1.52 us (1%)
    pallas_call x1, Pallas kernels, on_device(): pl.pallas_call(kernel, out_shape=jax.ShapeDtypeStruct((ROUNDS, 32, 256),...  100 us

profile of v5, /device:TPU:32, one launch (start us, length us, event | category | flops | bytes accessed | tf_op | source)
XLA Modules:
  0.0 101.9 jit_solution(2900422648468430968)
XLA Ops:
  0.0 100.4 %shard_map.46 = f32[2,32,256]{2,1,0:T(8,128)} custom-call(bf16[3,16,16,256]{3,2,1,0:T(8,128)(2,1)} %bitcast.3, bf16[3,16,16,256]{3,2,1,0:T(8,128)(2,1)} %bitcast.4, s32[2,64]{1,0:T(2,128)} %pair_ref.1, s32[3]{0:T(128)} %freq_ref.1), custom_call_target="tpu_custom_call" | custom-call | tf_op jit(solution)/shard_map/pallas_call | solution.py:285
  100.4 1.5 %copy.5 = f32[32,2,256]{2,1,0:T(2,128)} copy(f32[32,2,256]{2,0,1:T(8,128)} %bitcast.5) | data formatting | bytes 131072 | tf_op jit(solution)/shard_map/transpose | solution.py:318
